TPU v7x, 128 devices: a whole 4x4x4 slice. The times are simulated.
128 devices in a mesh: phase: 4 (over y_lo, core), dp: 4 (over z), tensor: 8 (over x, y_hi).
Axes of the slice: x: 4, y: 4 (y_hi: 2, y_lo: 2; y = y_hi * 2 + y_lo), z: 4, core: 2. Of those that a mesh axis runs over, the one named last changes fastest.
Arguments:
- inputs: bfloat16 [4, 256, 8192], P(None, 'dp', 'tensor')
- seq_parts: int32 [4, 4, 6], P(None, 'dp'), may hold values from 1 to 32, 64 in all within a row
- norm_gain: float32 [4, 8192], P('phase'), may hold values from 0.4 to 2.5
- w_query: bfloat16 [4, 8192, 4096], P('phase', None, 'tensor')
- w_key: bfloat16 [4, 8192, 1024], P('phase', None, 'tensor')
- w_value: bfloat16 [4, 8192, 1024], P('phase', None, 'tensor'), may hold values from -0.0625 to 0.0625
- w_out: bfloat16 [4, 4096, 8192], P('phase', 'tensor'), may hold values from -0.375 to 0.375
Outputs:
- section_outputs: bfloat16 [4, 4, 256, 8192], P('phase', None, 'dp', 'tensor')
Inputs may be any that keep to these rules, and one draw needn't show every extreme that they name: `seq_parts`: the entries of each data row sum to 64, and each data row's largest entry is exactly half of 64.
All inputs are finite; a program needn't handle non-finite values.
Results may differ from a plain program's by a relative error of at most 0.04.
Values may be sent and summed in bfloat16 or wider, within the bound.
No kernel may reach another device: no remote copies, remote signals or barrier semaphores. Data moves between devices by JAX's collectives and lax.ppermute only.
A program may use at most 128 MiB of HBM per device.

v0:
```python
import math

import jax
import jax.numpy as jnp
from jax import lax
from jax.sharding import PartitionSpec as P

D = 8192
HD = 128


epsilon = 1e-05
theta_base = 10000.0


def from_behind(shard, axis, by):
    count = lax.axis_size(axis)
    pairs = [(i, i + by) for i in range(count) if 0 <= i + by < count]
    return lax.ppermute(shard, axis, pairs)


def row_layout(part_lengths, row_count):
    lengths = jnp.sum(part_lengths.reshape(-1, 3), axis=1)
    seq_ends = jnp.cumsum(lengths)
    seq_starts = seq_ends - lengths
    places = jnp.arange(row_count, dtype=jnp.int32)
    segment = jnp.sum((places[:, None] >= seq_ends[None, :]).astype(jnp.int32), axis=1)
    owners = jnp.arange(lengths.shape[0], dtype=jnp.int32)
    seq_first = jnp.sum(
        jnp.where(segment[:, None] == owners[None, :], seq_starts[None, :], 0), axis=1
    )
    return (segment, places - seq_first)


def rotate(projected, position):
    row_count = projected.shape[0]
    head_count = projected.shape[1] // HD
    half_size = HD // 2
    frequency = jnp.exp(
        jnp.arange(half_size, dtype=jnp.float32) * (-2.0 * math.log(theta_base) / HD)
    )
    angles = position.astype(jnp.float32)[:, None] * frequency[None, :]
    cosine = jnp.cos(angles)[:, None, :]
    sine_part = jnp.sin(angles)[:, None, :]
    split_heads = projected.reshape(row_count, head_count, HD)
    first_half = split_heads[..., :half_size]
    second_half = split_heads[..., half_size:]
    turned = jnp.concatenate(
        [
            first_half * cosine - second_half * sine_part,
            second_half * cosine + first_half * sine_part,
        ],
        axis=-1,
    )
    return turned.reshape(row_count, head_count * HD)


def attend(queries, keys, values, segment, position):
    row_count = queries.shape[0]
    kv_heads = keys.shape[1] // HD
    group_size = queries.shape[1] // keys.shape[1]
    query_heads = queries.reshape(row_count, kv_heads, group_size, HD)
    key_heads = keys.reshape(row_count, kv_heads, HD)
    value_heads = values.reshape(row_count, kv_heads, HD)
    scores = jnp.einsum(
        "qhgd,shd->hgqs", query_heads, key_heads, preferred_element_type=jnp.float32
    ) / math.sqrt(HD)
    allowed = (segment[:, None] == segment[None, :]) & (position[None, :] <= position[:, None])
    scores = jnp.where(allowed[None, None], scores, -1e30)
    peak = jnp.max(scores, axis=-1, keepdims=True)
    weights = jnp.exp(scores - peak)
    shares = (weights / jnp.sum(weights, axis=-1, keepdims=True)).astype(jnp.bfloat16)
    mixed = jnp.einsum("hgqs,shd->qhgd", shares, value_heads, preferred_element_type=jnp.float32)
    return mixed.reshape(row_count, -1).astype(jnp.bfloat16)


def heads_from(query_sum, key_sum, value_sum, segment, position):
    queries = rotate(query_sum, position).astype(jnp.bfloat16)
    keys = rotate(key_sum, position).astype(jnp.bfloat16)
    values = value_sum.astype(jnp.bfloat16)
    return attend(queries, keys, values, segment, position)


def full_section(current, gain_row, query_w, key_w, value_w, out_w, segment, position):
    wide_state = current.astype(jnp.float32)
    mean_square = jnp.sum(wide_state * wide_state, axis=1, keepdims=True) / D
    normed = (wide_state * lax.rsqrt(mean_square + epsilon) * gain_row[None, :]).astype(
        jnp.bfloat16
    )
    query_sum = jnp.dot(normed, query_w, preferred_element_type=jnp.float32)
    key_sum = jnp.dot(normed, key_w, preferred_element_type=jnp.float32)
    value_sum = jnp.dot(normed, value_w, preferred_element_type=jnp.float32)
    heads_out = heads_from(query_sum, key_sum, value_sum, segment, position)
    partial_sum = jnp.dot(heads_out, out_w, preferred_element_type=jnp.float32)
    head_total = lax.psum(partial_sum.astype(jnp.bfloat16), "tensor").astype(jnp.float32)
    return (wide_state + head_total).astype(jnp.bfloat16)


def on_device(inputs, seq_parts, norm_gain, w_query, w_key, w_value, w_out):
    phase_count = lax.axis_size("phase")
    phase_index = lax.axis_index("phase")
    micro_count = inputs.shape[0]
    share_width = inputs.shape[2]
    tick_count = micro_count + phase_count - 1
    gain_row = norm_gain[0]
    query_w = w_query[0]
    key_w = w_key[0]
    value_w = w_value[0]
    out_w = w_out[0]
    sources = lax.all_gather(inputs, "tensor", axis=2, tiled=True)
    carried = jnp.zeros_like(sources[0])
    results = jnp.zeros(inputs.shape, jnp.bfloat16)
    for tick_index in range(tick_count):
        micro_index = tick_index - phase_index
        is_valid = (micro_index >= 0) & (micro_index < micro_count)
        micro_slot = jnp.clip(micro_index, 0, micro_count - 1)
        arriving = sources[min(tick_index, micro_count - 1)]
        current = jnp.where(phase_index == 0, arriving, carried)
        part_lengths = lax.dynamic_index_in_dim(seq_parts, micro_slot, 0, keepdims=False)[0]
        segment, position = row_layout(part_lengths, current.shape[0])
        updated = full_section(current, gain_row, query_w, key_w, value_w, out_w, segment, position)
        own_part = lax.dynamic_slice_in_dim(
            updated, lax.axis_index("tensor") * share_width, share_width, 1
        )
        if tick_index + 1 < tick_count:
            carried = from_behind(updated, "phase", 1)
        previous = lax.dynamic_index_in_dim(results, micro_slot, 0, keepdims=False)
        results = lax.dynamic_update_index_in_dim(
            results, jnp.where(is_valid, own_part, previous), micro_slot, 0
        )
    return results[None]


def solution(mesh):
    placed = (
        P(None, "dp", "tensor"),
        P(None, "dp", None),
        P("phase", None),
        P("phase", None, "tensor"),
        P("phase", None, "tensor"),
        P("phase", None, "tensor"),
        P("phase", "tensor", None),
    )
    return jax.shard_map(
        on_device,
        mesh=mesh,
        in_specs=placed,
        out_specs=P("phase", None, "dp", "tensor"),
        check_vma=False,
    )
```

profile of v0, /device:TPU:9, one launch (start us, length us, event | category | flops | bytes accessed | tf_op | source)
XLA Modules:
  0.0 924.1 jit_solution(40304270913437109)
XLA Ops:
  7.3 11.4 %copy.71 = bf16[512,8192]{1,0:T(8,128)(2,1)} copy(bf16[512,8192]{0,1:T(8,128)(2,1)} %bitcast.480) | data formatting | bytes 16777216 | tf_op jit(solution)/shard_map/dot_general | solution.py:90
  26.9 55.4 %all-gather.2.cloned.1.call-done = bf16[4,64,8192]{2,1,0:T(8,128)(2,1)} async-done(((bf16[4,64,1024]{2,1,0:T(8,128)(2,1)}), bf16[4,64,8192]{2,1,0:T(8,128)(2,1)}) %all-gather.2.cloned.1.call-update) | async-done | bytes 4194320 | tf_op jit(solution)/shard_map/all_gather | solution.py:110
  83.9 2.5 fusion.82
  86.6 6.4 fusion.159
  95.5 5.9 convolution_convert_fusion.6
  101.5 82.2 %all-reduce.8.cloned.1.call-done = bf16[64,8192]{1,0:T(8,128)(2,1)} async-done(((bf16[64,8192]{1,0:T(8,128)(2,1)}), bf16[64,8192]{1,0:T(8,128)(2,1)}) %all-reduce.8.cloned.1.call-update) | async-done | bytes 1048592 | tf_op jit(solution)/shard_map/psum | solution.py:95
  187.1 7.9 collective-permute-done
  196.8 6.2 fusion.157
  207.8 5.9 convolution_convert_fusion.5
  213.8 93.3 %all-reduce.10.cloned.1.call-done = bf16[64,8192]{1,0:T(8,128)(2,1)} async-done(((bf16[64,8192]{1,0:T(8,128)(2,1)}), bf16[64,8192]{1,0:T(8,128)(2,1)}) %all-reduce.10.cloned.1.call-update) | async-done | bytes 1048592 | tf_op jit(solution)/shard_map/psum | solution.py:95
  310.0 8.1 collective-permute-done.1
  319.8 6.2 fusion.155
  330.8 6.0 convolution_convert_fusion.4
  336.9 93.3 %all-reduce.12.cloned.1.call-done = bf16[64,8192]{1,0:T(8,128)(2,1)} async-done(((bf16[64,8192]{1,0:T(8,128)(2,1)}), bf16[64,8192]{1,0:T(8,128)(2,1)}) %all-reduce.12.cloned.1.call-update) | async-done | bytes 1048592 | tf_op jit(solution)/shard_map/psum | solution.py:95
  433.3 7.9 collective-permute-done.2
  442.9 6.2 fusion.153
  453.2 6.0 convolution_convert_fusion.3
  459.2 93.3 %all-reduce.14.cloned.1.call-done = bf16[64,8192]{1,0:T(8,128)(2,1)} async-done(((bf16[64,8192]{1,0:T(8,128)(2,1)}), bf16[64,8192]{1,0:T(8,128)(2,1)}) %all-reduce.14.cloned.1.call-update) | async-done | bytes 1048592 | tf_op jit(solution)/shard_map/psum | solution.py:95
  555.4 8.1 collective-permute-done.3
  565.2 6.2 fusion.151
  573.4 6.0 convolution_convert_fusion.2
  579.5 93.3 %all-reduce.16.cloned.1.call-done = bf16[64,8192]{1,0:T(8,128)(2,1)} async-done(((bf16[64,8192]{1,0:T(8,128)(2,1)}), bf16[64,8192]{1,0:T(8,128)(2,1)}) %all-reduce.16.cloned.1.call-update) | async-done | bytes 1048592 | tf_op jit(solution)/shard_map/psum | solution.py:95
  676.0 7.8 collective-permute-done.4
  685.5 6.2 fusion.149
  693.7 6.0 convolution_convert_fusion.1
  699.8 93.4 %all-reduce.18.cloned.1.call-done = bf16[64,8192]{1,0:T(8,128)(2,1)} async-done(((bf16[64,8192]{1,0:T(8,128)(2,1)}), bf16[64,8192]{1,0:T(8,128)(2,1)}) %all-reduce.18.cloned.1.call-update) | async-done | bytes 1048592 | tf_op jit(solution)/shard_map/psum | solution.py:95
  793.2 2.5 fusion.32
  799.9 5.6 collective-permute-done.5
  805.5 2.0 multiply_reduce_fusion
  807.5 6.2 fusion.147
  815.7 5.9 convolution_convert_fusion
  834.2 80.9 %all-reduce.20.cloned.1.call-done = bf16[64,8192]{1,0:T(8,128)(2,1)} async-done(((bf16[64,8192]{1,0:T(8,128)(2,1)}), bf16[64,8192]{1,0:T(8,128)(2,1)}) %all-reduce.20.cloned.1.call-update) | async-done | bytes 1048592 | tf_op jit(solution)/shard_map/psum | solution.py:95
  (247 shorter events, 74.9 us)
Async XLA Ops:
  6.5 86.9 %copy-start = (bf16[1,8192,128]{2,1,0:T(8,128)(2,1)S(1)}, bf16[1,8192,128]{2,1,0:T(8,128)(2,1)}, u32[]{:S(2)}) copy-start(bf16[1,8192,128]{2,1,0:T(8,128)(2,1)} %param.12) | copy-start | bytes 6291460
  6.5 75.7 %all-gather.2.cloned.1.call-start = ((), (), s32[]{:S(2)}) async-start(), calls=%async_computation | async-start | bytes 4718592 | tf_op jit(solution)/shard_map/all_gather | solution.py:110
  7.3 176.4 %all-reduce.8.cloned.1.call-start = ((), (), s32[]{:S(2)}) async-start(), calls=%async_computation.1 | async-start | bytes 2097152 | tf_op jit(solution)/shard_map/psum | solution.py:95
  7.3 11.4 %copy-start.11 = (s32[4,1,6]{2,1,0:T(1,128)S(1)}, s32[4,1,6]{2,1,0:T(1,128)}, u32[]{:S(2)}) copy-start(s32[4,1,6]{2,1,0:T(1,128)} %param.8) | copy-start | bytes 292
  7.3 76.6 %copy-start.2 = (f32[1,8192]{1,0:T(1,128)S(1)}, f32[1,8192]{1,0:T(1,128)}, u32[]{:S(2)}) copy-start(f32[1,8192]{1,0:T(1,128)} %param.9) | copy-start | bytes 98308
  23.2 63.2 %copy-start.16 = (f32[64]{0:T(128)}, f32[64]{0:T(128)S(1)}, u32[]{:S(2)}) copy-start(f32[64]{0:T(128)S(1)} %get-tuple-element.67) | copy-start | bytes 772
  23.2 63.2 %copy-start.26 = (f32[64]{0:T(128)}, f32[64]{0:T(128)S(1)}, u32[]{:S(2)}) copy-start(f32[64]{0:T(128)S(1)} %get-tuple-element.89) | copy-start | bytes 772
  23.7 62.7 %copy-start.24 = (f32[64]{0:T(128)}, f32[64]{0:T(128)S(1)}, u32[]{:S(2)}) copy-start(f32[64]{0:T(128)S(1)} %get-tuple-element.87) | copy-start | bytes 772
  24.3 62.1 %copy-start.22 = (f32[64]{0:T(128)}, f32[64]{0:T(128)S(1)}, u32[]{:S(2)}) copy-start(f32[64]{0:T(128)S(1)} %get-tuple-element.85) | copy-start | bytes 772
  24.8 61.6 %copy-start.20 = (f32[64]{0:T(128)}, f32[64]{0:T(128)S(1)}, u32[]{:S(2)}) copy-start(f32[64]{0:T(128)S(1)} %get-tuple-element.83) | copy-start | bytes 772
  25.3 61.1 %copy-start.18 = (f32[64]{0:T(128)}, f32[64]{0:T(128)S(1)}, u32[]{:S(2)}) copy-start(f32[64]{0:T(128)S(1)} %get-tuple-element.81) | copy-start | bytes 772
  101.4 205.7 %all-reduce.10.cloned.1.call-start = ((), (), s32[]{:S(2)}) async-start(), calls=%async_computation.2 | async-start | bytes 2097152 | tf_op jit(solution)/shard_map/psum | solution.py:95
  185.6 9.5 %collective-permute-start = (bf16[64,8192]{1,0:T(8,128)(2,1)S(1)}, bf16[64,8192]{1,0:T(8,128)(2,1)S(1)}, u32[]{:S(2)}, u32[]{:S(2)}) collective-permute-start(bf16[64,8192]{1,0:T(8,128)(2,1)S(1)} %fusion.10), channel_id=1, source_target_pairs={{0,32},{32,64},{64,96},{1,33},{33,65},{65,97},{2,34},{34,66},{66,9... | collective-permute-start | bytes 3145736 | tf_op jit(solution)/shard_map/ppermute | solution.py:19
  196.8 6.2 copy-start.35
  213.7 96.2 %copy-start.15 = (s32[64]{0:T(128)S(1)}, s32[64]{0:T(128)}, u32[]{:S(2)}) copy-start(s32[64]{0:T(128)} %copy-done.14) | copy-start | bytes 772
  213.7 96.2 %copy-start.34 = (s32[64]{0:T(128)S(1)}, s32[64]{0:T(128)}, u32[]{:S(2)}) copy-start(s32[64]{0:T(128)} %get-tuple-element.86) | copy-start | bytes 772
  213.8 216.4 %all-reduce.12.cloned.1.call-start = ((), (), s32[]{:S(2)}) async-start(), calls=%async_computation.3 | async-start | bytes 2097152 | tf_op jit(solution)/shard_map/psum | solution.py:95
  308.6 9.5 %collective-permute-start.1 = (bf16[64,8192]{1,0:T(8,128)(2,1)S(1)}, bf16[64,8192]{1,0:T(8,128)(2,1)S(1)}, u32[]{:S(2)}, u32[]{:S(2)}) collective-permute-start(bf16[64,8192]{1,0:T(8,128)(2,1)S(1)} %fusion.16), channel_id=1, source_target_pairs={{0,32},{32,64},{64,96},{1,33},{33,65},{65,97},{2,34},{34,66},{66,9... | collective-permute-start | bytes 3145736 | tf_op jit(solution)/shard_map/ppermute | solution.py:19
  336.8 96.4 %copy-start.13 = (s32[64]{0:T(128)S(1)}, s32[64]{0:T(128)}, u32[]{:S(2)}) copy-start(s32[64]{0:T(128)} %copy-done.12) | copy-start | bytes 772
  336.8 96.4 %copy-start.33 = (s32[64]{0:T(128)S(1)}, s32[64]{0:T(128)}, u32[]{:S(2)}) copy-start(s32[64]{0:T(128)} %get-tuple-element.84) | copy-start | bytes 772
  336.8 215.7 %all-reduce.14.cloned.1.call-start = ((), (), s32[]{:S(2)}) async-start(), calls=%async_computation.4 | async-start | bytes 2097152 | tf_op jit(solution)/shard_map/psum | solution.py:95
  431.7 9.5 %collective-permute-start.2 = (bf16[64,8192]{1,0:T(8,128)(2,1)S(1)}, bf16[64,8192]{1,0:T(8,128)(2,1)S(1)}, u32[]{:S(2)}, u32[]{:S(2)}) collective-permute-start(bf16[64,8192]{1,0:T(8,128)(2,1)S(1)} %fusion.20), channel_id=1, source_target_pairs={{0,32},{32,64},{64,96},{1,33},{33,65},{65,97},{2,34},{34,66},{66,9... | collective-permute-start | bytes 3145736 | tf_op jit(solution)/shard_map/ppermute | solution.py:19
  459.2 96.2 %copy-start.32 = (s32[64]{0:T(128)S(1)}, s32[64]{0:T(128)}, u32[]{:S(2)}) copy-start(s32[64]{0:T(128)} %get-tuple-element.82) | copy-start | bytes 772
  459.2 213.7 %all-reduce.16.cloned.1.call-start = ((), (), s32[]{:S(2)}) async-start(), calls=%async_computation.5 | async-start | bytes 2097152 | tf_op jit(solution)/shard_map/psum | solution.py:95
  554.0 9.5 %collective-permute-start.3 = (bf16[64,8192]{1,0:T(8,128)(2,1)S(1)}, bf16[64,8192]{1,0:T(8,128)(2,1)S(1)}, u32[]{:S(2)}, u32[]{:S(2)}) collective-permute-start(bf16[64,8192]{1,0:T(8,128)(2,1)S(1)} %fusion.24), channel_id=1, source_target_pairs={{0,32},{32,64},{64,96},{1,33},{33,65},{65,97},{2,34},{34,66},{66,9... | collective-permute-start | bytes 3145736 | tf_op jit(solution)/shard_map/ppermute | solution.py:19
  579.4 96.4 %copy-start.31 = (s32[64]{0:T(128)S(1)}, s32[64]{0:T(128)}, u32[]{:S(2)}) copy-start(s32[64]{0:T(128)} %get-tuple-element.80) | copy-start | bytes 772
  579.5 213.7 %all-reduce.18.cloned.1.call-start = ((), (), s32[]{:S(2)}) async-start(), calls=%async_computation.6 | async-start | bytes 2097152 | tf_op jit(solution)/shard_map/psum | solution.py:95
  674.3 9.5 %collective-permute-start.4 = (bf16[64,8192]{1,0:T(8,128)(2,1)S(1)}, bf16[64,8192]{1,0:T(8,128)(2,1)S(1)}, u32[]{:S(2)}, u32[]{:S(2)}) collective-permute-start(bf16[64,8192]{1,0:T(8,128)(2,1)S(1)} %fusion.28), channel_id=1, source_target_pairs={{0,32},{32,64},{64,96},{1,33},{33,65},{65,97},{2,34},{34,66},{66,9... | collective-permute-start | bytes 3145736 | tf_op jit(solution)/shard_map/ppermute | solution.py:19
  699.7 97.3 %copy-start.29 = (s32[64]{0:T(128)S(1)}, s32[64]{0:T(128)}, u32[]{:S(2)}) copy-start(s32[64]{0:T(128)} %copy-done.28) | copy-start | bytes 772
  699.7 97.3 %copy-start.30 = (s32[64]{0:T(128)S(1)}, s32[64]{0:T(128)}, u32[]{:S(2)}) copy-start(s32[64]{0:T(128)} %get-tuple-element.66) | copy-start | bytes 772
  699.8 215.3 %all-reduce.20.cloned.1.call-start = ((), (), s32[]{:S(2)}) async-start(), calls=%async_computation.7 | async-start | bytes 2097152 | tf_op jit(solution)/shard_map/psum | solution.py:95
  795.7 9.8 %collective-permute-start.5 = (bf16[64,8192]{1,0:T(8,128)(2,1)}, bf16[64,8192]{1,0:T(8,128)(2,1)}, u32[]{:S(2)}, u32[]{:S(2)}) collective-permute-start(bf16[64,8192]{1,0:T(8,128)(2,1)} %fusion.32), channel_id=1, source_target_pairs={{0,32},{32,64},{64,96},{1,33},{33,65},{65,97},{2,34},{34,66},{66,9... | collective-permute-start | bytes 3145736 | tf_op jit(solution)/shard_map/ppermute | solution.py:19
  (26 other events, 71.7 us)
Sparse Core Ops, SparseCore 0:
  9.7 72.5 all-gather.1
  101.5 82.1 all-reduce.7
  213.9 93.1 all-reduce.9
  336.9 93.1 all-reduce.11
  459.3 93.1 all-reduce.13
  579.6 93.2 all-reduce.15
  699.9 93.2 all-reduce.17
  821.8 93.1 all-reduce.19
where the time goes:
time: 938 us; the launch traced here: 924 us
  waiting for transfers between devices  731 us (78%)
  matrix products  103 us (11%)
  other arithmetic  45.2 us (5%)
  local copies, waits for them, and re-layouts  21.1 us (2%)
  between operations  15 us (2%)
    psum x7, waiting for transfers between devices, full_section(): lax.psum(partial_sum.astype(jnp.bfloat16), 'tensor').astype(jnp.float32)  630 us
    all_gather x1, waiting for transfers between devices, on_device(): sources = lax.all_gather(inputs, 'tensor', axis=2, tiled=True)  55.4 us
    ppermute x6, waiting for transfers between devices, from_behind(): return lax.ppermute(shard, axis, pairs)  45.4 us
    dot_general x7, matrix products, full_section(): query_sum = jnp.dot(normed, query_w, preferred_element_type=jnp.float32)  43.6 us
    dot_general x7, matrix products, full_section(): partial_sum = jnp.dot(heads_out, out_w, preferred_element_type=jnp.float32)  41.7 us
  transfers between devices with their start and end apart: 14, of which 14 were waited for; matrix products, arithmetic and copies ran while one was open for 4% of the time, Pallas kernels for 0%

commit v1 on v0

v1 whole, which is shorter than its diff:
```python
import math

import jax
import jax.numpy as jnp
from jax import lax
from jax.experimental import pallas as pl
from jax.experimental.pallas import tpu as pltpu
from jax.sharding import PartitionSpec as P

D = 8192
HD = 128
QF = 512
KF = 128
ROWS = 64
CHUNK = 1024
MICRO = 4
PEERS = 8
epsilon = 1e-05
theta_base = 10000.0

OFFSETS = [(2, 1), (2, 0), (1, 1), (3, 1), (1, 0), (3, 0), (0, 1), (0, 0)]


def moved(place, offset):
    x, y = place // 2, place % 2
    return ((x + offset[0]) % 4) * 2 + (y + offset[1]) % 2


def shift(value, offset, from_phase, to_phase):
    pairs = [(from_phase * PEERS + t, to_phase * PEERS + moved(t, offset)) for t in range(PEERS)]
    return lax.ppermute(value, ("phase", "tensor"), pairs)


def heads_kernel(
    source_ref, first_ref, cos_ref, sin_ref, gain_ref, *refs
):
    chunks = refs[:PEERS]
    query_hbm, key_hbm, value_hbm, out_ref = refs[PEERS:PEERS + 4]
    query_w, key_w, value_w, total, squares, copied = refs[PEERS + 4:]
    rows = out_ref.shape[0]

    def copies(j):
        begin = pl.multiple_of(source_ref[j] * CHUNK, CHUNK)
        held = pl.ds(j * CHUNK, CHUNK)
        return [
            pltpu.make_async_copy(query_hbm.at[pl.ds(begin, CHUNK)], query_w.at[held], copied.at[j, 0]),
            pltpu.make_async_copy(key_hbm.at[pl.ds(begin, CHUNK)], key_w.at[held], copied.at[j, 1]),
            pltpu.make_async_copy(value_hbm.at[pl.ds(begin, CHUNK)], value_w.at[held], copied.at[j, 2]),
        ]

    for j in range(PEERS):
        for copy in copies(j):
            copy.start()
    for j in range(PEERS):
        wide = chunks[j][...].astype(jnp.float32)
        gain = gain_ref[pl.ds(source_ref[j], 1), :]
        scaled = (wide * gain).astype(jnp.bfloat16)
        square = jnp.sum(wide * wide, axis=1, keepdims=True)
        for copy in copies(j):
            copy.wait()
        held = slice(j * CHUNK, (j + 1) * CHUNK)
        parts = [
            (slice(0, QF), query_w), (slice(QF, QF + KF), key_w), (slice(QF + KF, QF + 2 * KF), value_w)
        ]
        for columns, weight in parts:
            term = jnp.dot(scaled, weight[held, :], preferred_element_type=jnp.float32)
            if j == 0:
                total[:, columns] = term
            else:
                total[:, columns] += term
        if j == 0:
            squares[...] = square
        else:
            squares[...] += square
    scale = lax.rsqrt(squares[...] / D + epsilon)
    cosine = cos_ref[...]
    sine = sin_ref[...]

    def turned(part):
        part = part * scale
        return (part * cosine + pltpu.roll(part, HD // 2, 1) * sine).astype(jnp.bfloat16)

    queries = [turned(total[:, i * HD:(i + 1) * HD]) for i in range(QF // HD)]
    keys = turned(total[:, QF:QF + KF])
    values = (total[:, QF + KF:] * scale).astype(jnp.bfloat16)
    heads = QF // HD
    row = lax.broadcasted_iota(jnp.int32, (heads * ROWS, ROWS), 0) % ROWS
    column = lax.broadcasted_iota(jnp.int32, (heads * ROWS, ROWS), 1)
    for m in range(rows // ROWS):
        own = slice(m * ROWS, (m + 1) * ROWS)
        first = first_ref[m]
        query = jnp.concatenate([q[own] for q in queries], axis=0)
        scores = lax.dot_general(
            query, keys[own], (((1,), (1,)), ((), ())), preferred_element_type=jnp.float32
        ) / math.sqrt(HD)
        allowed = (column <= row) & ((row < first) | (column >= first))
        scores = jnp.where(allowed, scores, -1e30)
        weights = jnp.exp(scores - jnp.max(scores, axis=1, keepdims=True))
        shares = (weights / jnp.sum(weights, axis=1, keepdims=True)).astype(jnp.bfloat16)
        mixed = jnp.dot(shares, values[own], preferred_element_type=jnp.float32).astype(jnp.bfloat16)
        for i in range(heads):
            out_ref[own, i * HD:(i + 1) * HD] = mixed[i * ROWS:(i + 1) * ROWS]


def heads_call(source, first, cosine, sine, gain, chunks, query_w, key_w, value_w):
    rows = chunks[0].shape[0]
    vmem = pl.BlockSpec(memory_space=pltpu.VMEM)
    smem = pl.BlockSpec(memory_space=pltpu.SMEM)
    hbm = pl.BlockSpec(memory_space=pl.ANY)
    return pl.pallas_call(
        heads_kernel,
        out_shape=jax.ShapeDtypeStruct((rows, QF), jnp.bfloat16),
        in_specs=[smem, smem, vmem, vmem, vmem] + [vmem] * PEERS + [hbm] * 3,
        out_specs=vmem,
        scratch_shapes=[
            pltpu.VMEM((D, QF), jnp.bfloat16),
            pltpu.VMEM((D, KF), jnp.bfloat16),
            pltpu.VMEM((D, KF), jnp.bfloat16),
            pltpu.VMEM((rows, QF + 2 * KF), jnp.float32),
            pltpu.VMEM((rows, 1), jnp.float32),
            pltpu.SemaphoreType.DMA((PEERS, 3)),
        ],
        compiler_params=pltpu.CompilerParams(vmem_limit_bytes=40 * 2**20),
        cost_estimate=pl.CostEstimate(
            flops=2 * rows * D * (QF + 2 * KF), bytes_accessed=2 * D * (QF + 2 * KF), transcendentals=0
        ),
        name="heads",
    )(source, first, cosine, sine, gain, *chunks, query_w, key_w, value_w)


def terms_kernel(target_ref, heads_ref, weight_hbm, *refs):
    count = len(refs) - 2
    outs, weight, copied = refs[:count], refs[count], refs[count + 1]

    def copy(j):
        begin = pl.multiple_of(target_ref[j] * CHUNK, CHUNK)
        return pltpu.make_async_copy(
            weight_hbm.at[:, pl.ds(begin, CHUNK)], weight.at[j], copied.at[j]
        )

    for j in range(count):
        copy(j).start()
    for j in range(count):
        copy(j).wait()
        outs[j][...] = jnp.dot(
            heads_ref[...], weight[j], preferred_element_type=jnp.float32
        ).astype(jnp.bfloat16)


def terms_call(target, heads_out, weight):
    rows = heads_out.shape[0]
    count = target.shape[0]
    vmem = pl.BlockSpec(memory_space=pltpu.VMEM)
    return pl.pallas_call(
        terms_kernel,
        out_shape=[jax.ShapeDtypeStruct((rows, CHUNK), jnp.bfloat16)] * count,
        in_specs=[pl.BlockSpec(memory_space=pltpu.SMEM), vmem, pl.BlockSpec(memory_space=pl.ANY)],
        out_specs=[vmem] * count,
        scratch_shapes=[
            pltpu.VMEM((count, QF, CHUNK), jnp.bfloat16),
            pltpu.SemaphoreType.DMA((count,)),
        ],
        compiler_params=pltpu.CompilerParams(vmem_limit_bytes=24 * 2**20),
        cost_estimate=pl.CostEstimate(
            flops=2 * rows * QF * CHUNK * count, bytes_accessed=2 * QF * CHUNK * count, transcendentals=0
        ),
        name="terms",
    )(target, heads_out, weight)


def places(seq_parts):
    first = jnp.sum(seq_parts[:, 0, :3], axis=1)
    row = jnp.arange(ROWS, dtype=jnp.int32)[None, :]
    position = jnp.where(row < first[:, None], row, row - first[:, None]).reshape(-1)
    half = HD // 2
    frequency = jnp.exp(
        jnp.arange(half, dtype=jnp.float32) * (-2.0 * math.log(theta_base) / HD)
    )
    angles = position.astype(jnp.float32)[:, None] * frequency[None, :]
    cosine, sine = jnp.cos(angles), jnp.sin(angles)
    return (
        first,
        jnp.concatenate([cosine, cosine], axis=1),
        jnp.concatenate([-sine, sine], axis=1),
    )


def on_device(inputs, seq_parts, norm_gain, w_query, w_key, w_value, w_out):
    phase_count = lax.axis_size("phase")
    phase_index = lax.axis_index("phase")
    me = lax.axis_index("tensor")
    x, y = me // 2, me % 2
    source = jnp.stack([((x - dx) % 4) * 2 + (y - dy) % 2 for dx, dy in OFFSETS]).astype(jnp.int32)
    target = jnp.stack([((x + dx) % 4) * 2 + (y + dy) % 2 for dx, dy in OFFSETS]).astype(jnp.int32)
    first, cosine, sine = places(seq_parts)
    gain = norm_gain.reshape(PEERS, CHUNK)
    own = inputs.reshape(MICRO * ROWS, CHUNK)
    result = jnp.zeros_like(own)
    for phase in range(phase_count):
        if phase == 0:
            chunks = [shift(own, offset, 0, 0) for offset in OFFSETS[:-1]] + [own]
        else:
            chunks = [shift(own, offset, phase - 1, phase) for offset in OFFSETS]
        heads_out = heads_call(
            source, first, cosine, sine, gain, chunks, w_query[0], w_key[0], w_value[0]
        )
        terms = terms_call(target, heads_out, w_out[0])
        arrived = [shift(term, offset, phase, phase) for term, offset in zip(terms[:-1], OFFSETS[:-1])]
        head_total = terms[-1].astype(jnp.float32)
        for term in arrived:
            head_total = head_total + term.astype(jnp.float32)
        own = (chunks[-1].astype(jnp.float32) + head_total).astype(jnp.bfloat16)
        result = jnp.where(phase_index == phase, own, result)
    return result.reshape(1, MICRO, ROWS, CHUNK)


def solution(mesh):
    placed = (
        P(None, "dp", "tensor"),
        P(None, "dp", None),
        P("phase", None),
        P("phase", None, "tensor"),
        P("phase", None, "tensor"),
        P("phase", None, "tensor"),
        P("phase", "tensor", None),
    )
    return jax.shard_map(
        on_device,
        mesh=mesh,
        in_specs=placed,
        out_specs=P("phase", None, "dp", "tensor"),
        check_vma=False,
    )
```

time: 938 us -> 477 us (0.51)
  waiting for transfers between devices: 731 us -> 18.1 us
  starting transfers between devices: 8.66 us -> 373 us
  matrix products: 103 us -> 0 us
  Pallas kernels: 0 us -> 58.9 us
  other arithmetic: 45.2 us -> 10.2 us
  local copies, waits for them, and re-layouts: 21.1 us -> 6.16 us
  between operations: 15 us -> 1.71 us
    psum x7 -> x0, waiting for transfers between devices: 630 us -> none  [full_section(): lax.psum(partial_sum.astype(jnp.bfloat16), 'tensor').astype(jnp.float32)]
    ppermute x6 -> x59, starting transfers between devices: 8.38 us -> 373 us  [shift(): return lax.ppermute(value, ('phase', 'tensor'), pairs)]
    dot_general x35 -> x0, matrix products: 103 us -> none  [the longest x7 43.6 us: full_section(): query_sum = jnp.dot(normed, query_w, preferred_element_type=jnp.float32)]
    pallas_call x0 -> x8, Pallas kernels: none -> 58.9 us  [the longest x4 35.7 us: heads_call(): pl.pallas_call(heads_kernel, out_shape=jax.ShapeDtypeStruct((rows, QF), j...]
    all_gather x1 -> x0, waiting for transfers between devices: 55.4 us -> none  [on_device(): sources = lax.all_gather(inputs, 'tensor', axis=2, tiled=True)]
    ppermute x6 -> x59, waiting for transfers between devices: 45.4 us -> 18.1 us  [shift(): return lax.ppermute(value, ('phase', 'tensor'), pairs)]
    reduce_sum x32 -> x1, other arithmetic: 15.4 us -> 0.84 us  [places(): first = jnp.sum(seq_parts[:, 0, :3], axis=1)]
    dot_general x1 -> x0, local copies, waits for them, and re-layouts: 11.4 us -> none  [full_section(): query_sum = jnp.dot(normed, query_w, preferred_element_type=jnp.float32)]
  transfers between devices with their start and end apart: 14 -> 59, of which waited for: 14 -> 2; matrix products, arithmetic and copies ran while one was open for 4% -> 1% of each run, Pallas kernels for 0% -> 0%
where the time goes in v1:
time: 477 us; the launch traced here: 468 us
  starting transfers between devices  373 us (78%)
  Pallas kernels  58.9 us (12%)
  waiting for transfers between devices  18.1 us (4%)
  other arithmetic  10.2 us (2%)
  local copies, waits for them, and re-layouts  6.16 us (1%)
    ppermute x59, starting transfers between devices, shift(): return lax.ppermute(value, ('phase', 'tensor'), pairs)  373 us
    pallas_call x4, Pallas kernels, heads_call(): pl.pallas_call(heads_kernel, out_shape=jax.ShapeDtypeStruct((rows, QF), j...  35.7 us
    pallas_call x4, Pallas kernels, terms_call(): pl.pallas_call(terms_kernel, out_shape=[jax.ShapeDtypeStruct((rows, CHUNK...  23.2 us
    ppermute x59, waiting for transfers between devices, shift(): return lax.ppermute(value, ('phase', 'tensor'), pairs)  18.1 us
  transfers between devices with their start and end apart: 59, of which 2 were waited for; matrix products, arithmetic and copies ran while one was open for 1% of the time, Pallas kernels for 0%

profile of v1, /device:TPU:9, one launch (start us, length us, event | category | flops | bytes accessed | tf_op | source)
XLA Modules:
  0.0 467.8 jit_solution(14973271657379882745)
XLA Ops:
  5.3 1.5 reduce.4
  9.2 1.7 copy-done
  10.9 1.6 copy-done.2
  12.5 1.0 copy-done.4
  13.6 9.1 %heads.4.heads_ref = bf16[256,512]{1,0:T(8,128)(2,1)S(1)} custom-call(s32[8]{0:T(128)S(1)} %stack.68.source_ref, s32[4]{0:T(128)S(1)} %slice_reduce_fusion.first_ref, f32[256,128]{1,0:T(8,128)S(1)} %get-tuple-element.72.cos_ref, f32[256,128]{1,0:T(8,128)S(1)} %get-tuple-element.73.sin_ref, f32[8,1024]{1,0:T(8,128)S(1)} %reshape.46.gain_ref, ...), custom_call_target="tpu_custom_call" | custom-call | flops 3221225472 | bytes 12582912 | tf_op jit(solution)/shard_map/heads/pallas_call | solution.py:110
  22.7 5.7 %terms.4 = (bf16[256,1024]{1,0:T(8,128)(2,1)S(1)}, bf16[256,1024]{1,0:T(8,128)(2,1)S(1)}, bf16[256,1024]{1,0:T(8,128)(2,1)S(1)}, bf16[256,1024]{1,0:T(8,128)(2,1...) custom-call(s32[8]{0:T(128)S(1)} %stack.60.target_ref, ...), custom_call_target="tpu_custom_call" | custom-call | flops 2147483648 | bytes 8388608 | tf_op jit(solution)/shard_map/terms/pallas_call | solution.py:154
  33.6 1.0 add_convert_fusion.3
  40.4 8.9 %heads.5.heads_ref = bf16[256,512]{1,0:T(8,128)(2,1)S(1)} custom-call(s32[8]{0:T(128)S(1)} %stack.68.source_ref, s32[4]{0:T(128)S(1)} %slice_reduce_fusion.first_ref, f32[256,128]{1,0:T(8,128)S(1)} %get-tuple-element.72.cos_ref, f32[256,128]{1,0:T(8,128)S(1)} %get-tuple-element.73.sin_ref, f32[8,1024]{1,0:T(8,128)S(1)} %reshape.46.gain_ref, ...), custom_call_target="tpu_custom_call" | custom-call | flops 3221225472 | bytes 12582912 | tf_op jit(solution)/shard_map/heads/pallas_call | solution.py:110
  49.3 5.7 %terms.5 = (bf16[256,1024]{1,0:T(8,128)(2,1)S(1)}, bf16[256,1024]{1,0:T(8,128)(2,1)S(1)}, bf16[256,1024]{1,0:T(8,128)(2,1)S(1)}, bf16[256,1024]{1,0:T(8,128)(2,1...) custom-call(s32[8]{0:T(128)S(1)} %stack.60.target_ref, ...), custom_call_target="tpu_custom_call" | custom-call | flops 2147483648 | bytes 8388608 | tf_op jit(solution)/shard_map/terms/pallas_call | solution.py:154
  66.9 8.9 %heads.6.heads_ref = bf16[256,512]{1,0:T(8,128)(2,1)S(1)} custom-call(s32[8]{0:T(128)S(1)} %stack.68.source_ref, s32[4]{0:T(128)S(1)} %slice_reduce_fusion.first_ref, f32[256,128]{1,0:T(8,128)S(1)} %get-tuple-element.72.cos_ref, f32[256,128]{1,0:T(8,128)S(1)} %get-tuple-element.73.sin_ref, f32[8,1024]{1,0:T(8,128)S(1)} %reshape.46.gain_ref, ...), custom_call_target="tpu_custom_call" | custom-call | flops 3221225472 | bytes 12582912 | tf_op jit(solution)/shard_map/heads/pallas_call | solution.py:110
  75.8 5.7 %terms.6 = (bf16[256,1024]{1,0:T(8,128)(2,1)S(1)}, bf16[256,1024]{1,0:T(8,128)(2,1)S(1)}, bf16[256,1024]{1,0:T(8,128)(2,1)S(1)}, bf16[256,1024]{1,0:T(8,128)(2,1...) custom-call(s32[8]{0:T(128)S(1)} %stack.60.target_ref, ...), custom_call_target="tpu_custom_call" | custom-call | flops 2147483648 | bytes 8388608 | tf_op jit(solution)/shard_map/terms/pallas_call | solution.py:154
  83.6 176.6 %collective-permute-start.40 = (bf16[256,1024]{1,0:T(8,128)(2,1)S(1)}, bf16[256,1024]{1,0:T(8,128)(2,1)S(1)}, u32[]{:S(2)}, u32[]{:S(2)}) collective-permute-start(bf16[256,1024]{1,0:T(8,128)(2,1)S(1)} %get-tuple-element.57), channel_id=1, source_target_pairs={{64,71},{65,70},{66,65},{67,64},{68,67},{69,66},{70,69},{71,68},{7... | collective-permute-start | bytes 1572872 | tf_op jit(solution)/shard_map/ppermute | solution.py:31
  263.7 25.9 %collective-permute-start.44 = (bf16[256,1024]{1,0:T(8,128)(2,1)S(1)}, bf16[256,1024]{1,0:T(8,128)(2,1)S(1)}, u32[]{:S(2)}, u32[]{:S(2)}) collective-permute-start(bf16[256,1024]{1,0:T(8,128)(2,1)S(1)} %add_convert_fusion.1), channel_id=1, source_target_pairs={{64,96},{65,97},{66,98},{67,99},{68,100},{69,101},{70,102},{71,103... | collective-permute-start | bytes 1572872 | tf_op jit(solution)/shard_map/ppermute | solution.py:31
  289.7 10.0 %collective-permute-start.45 = (bf16[256,1024]{1,0:T(8,128)(2,1)S(1)}, bf16[256,1024]{1,0:T(8,128)(2,1)S(1)}, u32[]{:S(2)}, u32[]{:S(2)}) collective-permute-start(bf16[256,1024]{1,0:T(8,128)(2,1)S(1)} %add_convert_fusion.1), channel_id=1, source_target_pairs={{64,101},{65,100},{66,103},{67,102},{68,97},{69,96},{70,99},{71,98... | collective-permute-start | bytes 1572872 | tf_op jit(solution)/shard_map/ppermute | solution.py:31
  299.6 10.0 %collective-permute-start.46 = (bf16[256,1024]{1,0:T(8,128)(2,1)S(1)}, bf16[256,1024]{1,0:T(8,128)(2,1)S(1)}, u32[]{:S(2)}, u32[]{:S(2)}) collective-permute-start(bf16[256,1024]{1,0:T(8,128)(2,1)S(1)} %add_convert_fusion.1), channel_id=1, source_target_pairs={{64,100},{65,101},{66,102},{67,103},{68,96},{69,97},{70,98},{71,99... | collective-permute-start | bytes 1572872 | tf_op jit(solution)/shard_map/ppermute | solution.py:31
  309.6 10.0 %collective-permute-start.47 = (bf16[256,1024]{1,0:T(8,128)(2,1)S(1)}, bf16[256,1024]{1,0:T(8,128)(2,1)S(1)}, u32[]{:S(2)}, u32[]{:S(2)}) collective-permute-start(bf16[256,1024]{1,0:T(8,128)(2,1)S(1)} %add_convert_fusion.1), channel_id=1, source_target_pairs={{64,99},{65,98},{66,101},{67,100},{68,103},{69,102},{70,97},{71,96... | collective-permute-start | bytes 1572872 | tf_op jit(solution)/shard_map/ppermute | solution.py:31
  319.6 10.0 %collective-permute-start.48 = (bf16[256,1024]{1,0:T(8,128)(2,1)S(1)}, bf16[256,1024]{1,0:T(8,128)(2,1)S(1)}, u32[]{:S(2)}, u32[]{:S(2)}) collective-permute-start(bf16[256,1024]{1,0:T(8,128)(2,1)S(1)} %add_convert_fusion.1), channel_id=1, source_target_pairs={{64,103},{65,102},{66,97},{67,96},{68,99},{69,98},{70,101},{71,100... | collective-permute-start | bytes 1572872 | tf_op jit(solution)/shard_map/ppermute | solution.py:31
  329.6 10.0 %collective-permute-start.49 = (bf16[256,1024]{1,0:T(8,128)(2,1)S(1)}, bf16[256,1024]{1,0:T(8,128)(2,1)S(1)}, u32[]{:S(2)}, u32[]{:S(2)}) collective-permute-start(bf16[256,1024]{1,0:T(8,128)(2,1)S(1)} %add_convert_fusion.1), channel_id=1, source_target_pairs={{64,98},{65,99},{66,100},{67,101},{68,102},{69,103},{70,96},{71,97... | collective-permute-start | bytes 1572872 | tf_op jit(solution)/shard_map/ppermute | solution.py:31
  339.6 10.0 %collective-permute-start.50 = (bf16[256,1024]{1,0:T(8,128)(2,1)S(1)}, bf16[256,1024]{1,0:T(8,128)(2,1)S(1)}, u32[]{:S(2)}, u32[]{:S(2)}) collective-permute-start(bf16[256,1024]{1,0:T(8,128)(2,1)S(1)} %add_convert_fusion.1), channel_id=1, source_target_pairs={{64,102},{65,103},{66,96},{67,97},{68,98},{69,99},{70,100},{71,101... | collective-permute-start | bytes 1572872 | tf_op jit(solution)/shard_map/ppermute | solution.py:31
  349.6 10.0 %collective-permute-start.51 = (bf16[256,1024]{1,0:T(8,128)(2,1)S(1)}, bf16[256,1024]{1,0:T(8,128)(2,1)S(1)}, u32[]{:S(2)}, u32[]{:S(2)}) collective-permute-start(bf16[256,1024]{1,0:T(8,128)(2,1)S(1)} %add_convert_fusion.1), channel_id=1, source_target_pairs={{64,97},{65,96},{66,99},{67,98},{68,101},{69,100},{70,103},{71,102... | collective-permute-start | bytes 1572872 | tf_op jit(solution)/shard_map/ppermute | solution.py:31
  359.6 9.5 %collective-permute-done.51.refs_6_ = bf16[256,1024]{1,0:T(8,128)(2,1)S(1)} collective-permute-done((bf16[256,1024]{1,0:T(8,128)(2,1)S(1)}, bf16[256,1024]{1,0:T(8,128)(2,1)S(1)}, u32[]{:S(2)}, u32[]{:S(2)}) %collective-permute-start.51) | collective-permute-done | bytes 524320 | tf_op jit(solution)/shard_map/ppermute | solution.py:31
  369.2 8.9 %heads.7.heads_ref = bf16[256,512]{1,0:T(8,128)(2,1)S(1)} custom-call(s32[8]{0:T(128)S(1)} %stack.68.source_ref, s32[4]{0:T(128)S(1)} %slice_reduce_fusion.first_ref, f32[256,128]{1,0:T(8,128)S(1)} %get-tuple-element.72.cos_ref, f32[256,128]{1,0:T(8,128)S(1)} %get-tuple-element.73.sin_ref, f32[8,1024]{1,0:T(8,128)S(1)} %reshape.46.gain_ref, ...), custom_call_target="tpu_custom_call" | custom-call | flops 3221225472 | bytes 12582912 | tf_op jit(solution)/shard_map/heads/pallas_call | solution.py:110
  378.1 6.1 %terms.7 = (bf16[256,1024]{1,0:T(8,128)(2,1)S(1)}, bf16[256,1024]{1,0:T(8,128)(2,1)S(1)}, bf16[256,1024]{1,0:T(8,128)(2,1)}, bf16[256,1024]{1,0:T(8,128)(2,1)S(1...) custom-call(s32[8]{0:T(128)S(1)} %stack.60.target_ref, ...), custom_call_target="tpu_custom_call" | custom-call | flops 2147483648 | bytes 8388608 | tf_op jit(solution)/shard_map/terms/pallas_call | solution.py:154
  384.1 8.9 %collective-permute-start.52 = (bf16[256,1024]{1,0:T(8,128)(2,1)S(1)}, bf16[256,1024]{1,0:T(8,128)(2,1)S(1)}, u32[]{:S(2)}, u32[]{:S(2)}) collective-permute-start(bf16[256,1024]{1,0:T(8,128)(2,1)S(1)} %get-tuple-element.62), channel_id=1, source_target_pairs={{96,101},{97,100},{98,103},{99,102},{100,97},{101,96},{102,99},{10... | collective-permute-start | bytes 1572872 | tf_op jit(solution)/shard_map/ppermute | solution.py:31
  393.0 9.7 %collective-permute-start.53 = (bf16[256,1024]{1,0:T(8,128)(2,1)S(1)}, bf16[256,1024]{1,0:T(8,128)(2,1)S(1)}, u32[]{:S(2)}, u32[]{:S(2)}) collective-permute-start(bf16[256,1024]{1,0:T(8,128)(2,1)S(1)} %get-tuple-element.63), channel_id=1, source_target_pairs={{96,100},{97,101},{98,102},{99,103},{100,96},{101,97},{102,98},{10... | collective-permute-start | bytes 1572872 | tf_op jit(solution)/shard_map/ppermute | solution.py:31
  402.8 9.7 %collective-permute-start.54 = (bf16[256,1024]{1,0:T(8,128)(2,1)}, bf16[256,1024]{1,0:T(8,128)(2,1)}, u32[]{:S(2)}, u32[]{:S(2)}) collective-permute-start(bf16[256,1024]{1,0:T(8,128)(2,1)} %get-tuple-element.64), channel_id=1, source_target_pairs={{96,99},{97,98},{98,101},{99,100},{100,103},{101,102},{102,97},{10... | collective-permute-start | bytes 1572872 | tf_op jit(solution)/shard_map/ppermute | solution.py:31
  412.5 10.3 %collective-permute-start.55 = (bf16[256,1024]{1,0:T(8,128)(2,1)S(1)}, bf16[256,1024]{1,0:T(8,128)(2,1)}, u32[]{:S(2)}, u32[]{:S(2)}) collective-permute-start(bf16[256,1024]{1,0:T(8,128)(2,1)S(1)} %get-tuple-element.65), channel_id=1, source_target_pairs={{96,103},{97,102},{98,97},{99,96},{100,99},{101,98},{102,101},{103... | collective-permute-start | bytes 1572872 | tf_op jit(solution)/shard_map/ppermute | solution.py:31
  422.8 10.3 %collective-permute-start.56 = (bf16[256,1024]{1,0:T(8,128)(2,1)S(1)}, bf16[256,1024]{1,0:T(8,128)(2,1)}, u32[]{:S(2)}, u32[]{:S(2)}) collective-permute-start(bf16[256,1024]{1,0:T(8,128)(2,1)S(1)} %get-tuple-element.66), channel_id=1, source_target_pairs={{96,98},{97,99},{98,100},{99,101},{100,102},{101,103},{102,96},{10... | collective-permute-start | bytes 1572872 | tf_op jit(solution)/shard_map/ppermute | solution.py:31
  433.2 10.3 %collective-permute-start.57 = (bf16[256,1024]{1,0:T(8,128)(2,1)S(1)}, bf16[256,1024]{1,0:T(8,128)(2,1)}, u32[]{:S(2)}, u32[]{:S(2)}) collective-permute-start(bf16[256,1024]{1,0:T(8,128)(2,1)S(1)} %get-tuple-element.67), channel_id=1, source_target_pairs={{96,102},{97,103},{98,96},{99,97},{100,98},{101,99},{102,100},{103... | collective-permute-start | bytes 1572872 | tf_op jit(solution)/shard_map/ppermute | solution.py:31
  444.3 10.3 %collective-permute-start.58 = (bf16[256,1024]{1,0:T(8,128)(2,1)S(1)}, bf16[256,1024]{1,0:T(8,128)(2,1)}, u32[]{:S(2)}, u32[]{:S(2)}) collective-permute-start(bf16[256,1024]{1,0:T(8,128)(2,1)S(1)} %get-tuple-element.68), channel_id=1, source_target_pairs={{96,97},{97,96},{98,99},{99,98},{100,101},{101,100},{102,103},{103... | collective-permute-start | bytes 1572872 | tf_op jit(solution)/shard_map/ppermute | solution.py:31
  454.7 8.4 %collective-permute-done.58 = bf16[256,1024]{1,0:T(8,128)(2,1)} collective-permute-done((bf16[256,1024]{1,0:T(8,128)(2,1)S(1)}, bf16[256,1024]{1,0:T(8,128)(2,1)}, u32[]{:S(2)}, u32[]{:S(2)}) %collective-permute-start.58) | collective-permute-done | bytes 524320 | tf_op jit(solution)/shard_map/ppermute | solution.py:31
  463.1 4.2 fusion
  (137 shorter events, 36.0 us)
Async XLA Ops:
  0.0 7.0 %collective-permute-start = (bf16[256,1024]{1,0:T(8,128)(2,1)}, bf16[256,1024]{1,0:T(8,128)(2,1)S(1)}, u32[]{:S(2)}, u32[]{:S(2)}) collective-permute-start(bf16[256,1024]{1,0:T(8,128)(2,1)} %bitcast.36), channel_id=1, source_target_pairs={{0,5},{1,4},{2,7},{3,6},{4,1},{5,0},{6,3},{7,2},{8,13},{9,12},{10,... | collective-permute-start | bytes 1572872 | tf_op jit(solution)/shard_map/ppermute | solution.py:31
  0.7 7.0 %collective-permute-start.1 = (bf16[256,1024]{1,0:T(8,128)(2,1)}, bf16[256,1024]{1,0:T(8,128)(2,1)S(1)}, u32[]{:S(2)}, u32[]{:S(2)}) collective-permute-start(bf16[256,1024]{1,0:T(8,128)(2,1)} %bitcast.37), channel_id=1, source_target_pairs={{0,4},{1,5},{2,6},{3,7},{4,0},{5,1},{6,2},{7,3},{8,12},{9,13},{10,... | collective-permute-start | bytes 1572872 | tf_op jit(solution)/shard_map/ppermute | solution.py:31
  1.4 7.7 %collective-permute-start.2 = (bf16[256,1024]{1,0:T(8,128)(2,1)}, bf16[256,1024]{1,0:T(8,128)(2,1)S(1)}, u32[]{:S(2)}, u32[]{:S(2)}) collective-permute-start(bf16[256,1024]{1,0:T(8,128)(2,1)} %bitcast.38), channel_id=1, source_target_pairs={{0,3},{1,2},{2,5},{3,4},{4,7},{5,6},{6,1},{7,0},{8,11},{9,10},{10,... | collective-permute-start | bytes 1572872 | tf_op jit(solution)/shard_map/ppermute | solution.py:31
  2.1 7.0 %collective-permute-start.3 = (bf16[256,1024]{1,0:T(8,128)(2,1)}, bf16[256,1024]{1,0:T(8,128)(2,1)S(1)}, u32[]{:S(2)}, u32[]{:S(2)}) collective-permute-start(bf16[256,1024]{1,0:T(8,128)(2,1)} %bitcast.39), channel_id=1, source_target_pairs={{0,7},{1,6},{2,1},{3,0},{4,3},{5,2},{6,5},{7,4},{8,15},{9,14},{10,... | collective-permute-start | bytes 1572872 | tf_op jit(solution)/shard_map/ppermute | solution.py:31
  2.8 6.4 %collective-permute-start.4 = (bf16[256,1024]{1,0:T(8,128)(2,1)}, bf16[256,1024]{1,0:T(8,128)(2,1)S(1)}, u32[]{:S(2)}, u32[]{:S(2)}) collective-permute-start(bf16[256,1024]{1,0:T(8,128)(2,1)} %bitcast.40), channel_id=1, source_target_pairs={{0,2},{1,3},{2,4},{3,5},{4,6},{5,7},{6,0},{7,1},{8,10},{9,11},{10,... | collective-permute-start | bytes 1572872 | tf_op jit(solution)/shard_map/ppermute | solution.py:31
  29.2 3.5 collective-permute-start.11
  29.9 3.7 collective-permute-start.12
  35.4 3.5 collective-permute-start.15
  36.1 3.5 collective-permute-start.16
  36.8 3.5 collective-permute-start.17
  56.4 3.7 collective-permute-start.24
  62.6 3.5 collective-permute-start.31
  63.3 3.5 collective-permute-start.32
  81.5 179.4 %collective-permute-start.37 = (bf16[256,1024]{1,0:T(8,128)(2,1)S(1)}, bf16[256,1024]{1,0:T(8,128)(2,1)S(1)}, u32[]{:S(2)}, u32[]{:S(2)}) collective-permute-start(bf16[256,1024]{1,0:T(8,128)(2,1)S(1)} %get-tuple-element.54), channel_id=1, source_target_pairs={{64,69},{65,68},{66,71},{67,70},{68,65},{69,64},{70,67},{71,66},{7... | collective-permute-start | bytes 1572872 | tf_op jit(solution)/shard_map/ppermute | solution.py:31
  82.2 179.5 %collective-permute-start.38 = (bf16[256,1024]{1,0:T(8,128)(2,1)S(1)}, bf16[256,1024]{1,0:T(8,128)(2,1)S(1)}, u32[]{:S(2)}, u32[]{:S(2)}) collective-permute-start(bf16[256,1024]{1,0:T(8,128)(2,1)S(1)} %get-tuple-element.55), channel_id=1, source_target_pairs={{64,68},{65,69},{66,70},{67,71},{68,64},{69,65},{70,66},{71,67},{7... | collective-permute-start | bytes 1572872 | tf_op jit(solution)/shard_map/ppermute | solution.py:31
  82.9 179.7 %collective-permute-start.39 = (bf16[256,1024]{1,0:T(8,128)(2,1)S(1)}, bf16[256,1024]{1,0:T(8,128)(2,1)S(1)}, u32[]{:S(2)}, u32[]{:S(2)}) collective-permute-start(bf16[256,1024]{1,0:T(8,128)(2,1)S(1)} %get-tuple-element.56), channel_id=1, source_target_pairs={{64,67},{65,66},{66,69},{67,68},{68,71},{69,70},{70,65},{71,64},{7... | collective-permute-start | bytes 1572872 | tf_op jit(solution)/shard_map/ppermute | solution.py:31
  83.6 179.0 %collective-permute-start.40 = (bf16[256,1024]{1,0:T(8,128)(2,1)S(1)}, bf16[256,1024]{1,0:T(8,128)(2,1)S(1)}, u32[]{:S(2)}, u32[]{:S(2)}) collective-permute-start(bf16[256,1024]{1,0:T(8,128)(2,1)S(1)} %get-tuple-element.57), channel_id=1, source_target_pairs={{64,71},{65,70},{66,65},{67,64},{68,67},{69,66},{70,69},{71,68},{7... | collective-permute-start | bytes 1572872 | tf_op jit(solution)/shard_map/ppermute | solution.py:31
  263.7 65.9 %collective-permute-start.44 = (bf16[256,1024]{1,0:T(8,128)(2,1)S(1)}, bf16[256,1024]{1,0:T(8,128)(2,1)S(1)}, u32[]{:S(2)}, u32[]{:S(2)}) collective-permute-start(bf16[256,1024]{1,0:T(8,128)(2,1)S(1)} %add_convert_fusion.1), channel_id=1, source_target_pairs={{64,96},{65,97},{66,98},{67,99},{68,100},{69,101},{70,102},{71,103... | collective-permute-start | bytes 1572872 | tf_op jit(solution)/shard_map/ppermute | solution.py:31
  289.7 50.0 %collective-permute-start.45 = (bf16[256,1024]{1,0:T(8,128)(2,1)S(1)}, bf16[256,1024]{1,0:T(8,128)(2,1)S(1)}, u32[]{:S(2)}, u32[]{:S(2)}) collective-permute-start(bf16[256,1024]{1,0:T(8,128)(2,1)S(1)} %add_convert_fusion.1), channel_id=1, source_target_pairs={{64,101},{65,100},{66,103},{67,102},{68,97},{69,96},{70,99},{71,98... | collective-permute-start | bytes 1572872 | tf_op jit(solution)/shard_map/ppermute | solution.py:31
  299.6 50.0 %collective-permute-start.46 = (bf16[256,1024]{1,0:T(8,128)(2,1)S(1)}, bf16[256,1024]{1,0:T(8,128)(2,1)S(1)}, u32[]{:S(2)}, u32[]{:S(2)}) collective-permute-start(bf16[256,1024]{1,0:T(8,128)(2,1)S(1)} %add_convert_fusion.1), channel_id=1, source_target_pairs={{64,100},{65,101},{66,102},{67,103},{68,96},{69,97},{70,98},{71,99... | collective-permute-start | bytes 1572872 | tf_op jit(solution)/shard_map/ppermute | solution.py:31
  309.6 50.0 %collective-permute-start.47 = (bf16[256,1024]{1,0:T(8,128)(2,1)S(1)}, bf16[256,1024]{1,0:T(8,128)(2,1)S(1)}, u32[]{:S(2)}, u32[]{:S(2)}) collective-permute-start(bf16[256,1024]{1,0:T(8,128)(2,1)S(1)} %add_convert_fusion.1), channel_id=1, source_target_pairs={{64,99},{65,98},{66,101},{67,100},{68,103},{69,102},{70,97},{71,96... | collective-permute-start | bytes 1572872 | tf_op jit(solution)/shard_map/ppermute | solution.py:31
  319.6 40.0 %collective-permute-start.48 = (bf16[256,1024]{1,0:T(8,128)(2,1)S(1)}, bf16[256,1024]{1,0:T(8,128)(2,1)S(1)}, u32[]{:S(2)}, u32[]{:S(2)}) collective-permute-start(bf16[256,1024]{1,0:T(8,128)(2,1)S(1)} %add_convert_fusion.1), channel_id=1, source_target_pairs={{64,103},{65,102},{66,97},{67,96},{68,99},{69,98},{70,101},{71,100... | collective-permute-start | bytes 1572872 | tf_op jit(solution)/shard_map/ppermute | solution.py:31
  329.6 30.0 %collective-permute-start.49 = (bf16[256,1024]{1,0:T(8,128)(2,1)S(1)}, bf16[256,1024]{1,0:T(8,128)(2,1)S(1)}, u32[]{:S(2)}, u32[]{:S(2)}) collective-permute-start(bf16[256,1024]{1,0:T(8,128)(2,1)S(1)} %add_convert_fusion.1), channel_id=1, source_target_pairs={{64,98},{65,99},{66,100},{67,101},{68,102},{69,103},{70,96},{71,97... | collective-permute-start | bytes 1572872 | tf_op jit(solution)/shard_map/ppermute | solution.py:31
  339.6 20.0 %collective-permute-start.50 = (bf16[256,1024]{1,0:T(8,128)(2,1)S(1)}, bf16[256,1024]{1,0:T(8,128)(2,1)S(1)}, u32[]{:S(2)}, u32[]{:S(2)}) collective-permute-start(bf16[256,1024]{1,0:T(8,128)(2,1)S(1)} %add_convert_fusion.1), channel_id=1, source_target_pairs={{64,102},{65,103},{66,96},{67,97},{68,98},{69,99},{70,100},{71,101... | collective-permute-start | bytes 1572872 | tf_op jit(solution)/shard_map/ppermute | solution.py:31
  349.6 19.6 %collective-permute-start.51 = (bf16[256,1024]{1,0:T(8,128)(2,1)S(1)}, bf16[256,1024]{1,0:T(8,128)(2,1)S(1)}, u32[]{:S(2)}, u32[]{:S(2)}) collective-permute-start(bf16[256,1024]{1,0:T(8,128)(2,1)S(1)} %add_convert_fusion.1), channel_id=1, source_target_pairs={{64,97},{65,96},{66,99},{67,98},{68,101},{69,100},{70,103},{71,102... | collective-permute-start | bytes 1572872 | tf_op jit(solution)/shard_map/ppermute | solution.py:31
  384.1 49.0 %collective-permute-start.52 = (bf16[256,1024]{1,0:T(8,128)(2,1)S(1)}, bf16[256,1024]{1,0:T(8,128)(2,1)S(1)}, u32[]{:S(2)}, u32[]{:S(2)}) collective-permute-start(bf16[256,1024]{1,0:T(8,128)(2,1)S(1)} %get-tuple-element.62), channel_id=1, source_target_pairs={{96,101},{97,100},{98,103},{99,102},{100,97},{101,96},{102,99},{10... | collective-permute-start | bytes 1572872 | tf_op jit(solution)/shard_map/ppermute | solution.py:31
  393.0 50.4 %collective-permute-start.53 = (bf16[256,1024]{1,0:T(8,128)(2,1)S(1)}, bf16[256,1024]{1,0:T(8,128)(2,1)S(1)}, u32[]{:S(2)}, u32[]{:S(2)}) collective-permute-start(bf16[256,1024]{1,0:T(8,128)(2,1)S(1)} %get-tuple-element.63), channel_id=1, source_target_pairs={{96,100},{97,101},{98,102},{99,103},{100,96},{101,97},{102,98},{10... | collective-permute-start | bytes 1572872 | tf_op jit(solution)/shard_map/ppermute | solution.py:31
  402.8 51.9 %collective-permute-start.54 = (bf16[256,1024]{1,0:T(8,128)(2,1)}, bf16[256,1024]{1,0:T(8,128)(2,1)}, u32[]{:S(2)}, u32[]{:S(2)}) collective-permute-start(bf16[256,1024]{1,0:T(8,128)(2,1)} %get-tuple-element.64), channel_id=1, source_target_pairs={{96,99},{97,98},{98,101},{99,100},{100,103},{101,102},{102,97},{10... | collective-permute-start | bytes 1572872 | tf_op jit(solution)/shard_map/ppermute | solution.py:31
  412.5 42.2 %collective-permute-start.55 = (bf16[256,1024]{1,0:T(8,128)(2,1)S(1)}, bf16[256,1024]{1,0:T(8,128)(2,1)}, u32[]{:S(2)}, u32[]{:S(2)}) collective-permute-start(bf16[256,1024]{1,0:T(8,128)(2,1)S(1)} %get-tuple-element.65), channel_id=1, source_target_pairs={{96,103},{97,102},{98,97},{99,96},{100,99},{101,98},{102,101},{103... | collective-permute-start | bytes 1572872 | tf_op jit(solution)/shard_map/ppermute | solution.py:31
  422.8 31.8 %collective-permute-start.56 = (bf16[256,1024]{1,0:T(8,128)(2,1)S(1)}, bf16[256,1024]{1,0:T(8,128)(2,1)}, u32[]{:S(2)}, u32[]{:S(2)}) collective-permute-start(bf16[256,1024]{1,0:T(8,128)(2,1)S(1)} %get-tuple-element.66), channel_id=1, source_target_pairs={{96,98},{97,99},{98,100},{99,101},{100,102},{101,103},{102,96},{10... | collective-permute-start | bytes 1572872 | tf_op jit(solution)/shard_map/ppermute | solution.py:31
  433.2 21.5 %collective-permute-start.57 = (bf16[256,1024]{1,0:T(8,128)(2,1)S(1)}, bf16[256,1024]{1,0:T(8,128)(2,1)}, u32[]{:S(2)}, u32[]{:S(2)}) collective-permute-start(bf16[256,1024]{1,0:T(8,128)(2,1)S(1)} %get-tuple-element.67), channel_id=1, source_target_pairs={{96,102},{97,103},{98,96},{99,97},{100,98},{101,99},{102,100},{103... | collective-permute-start | bytes 1572872 | tf_op jit(solution)/shard_map/ppermute | solution.py:31
  444.3 18.8 %collective-permute-start.58 = (bf16[256,1024]{1,0:T(8,128)(2,1)S(1)}, bf16[256,1024]{1,0:T(8,128)(2,1)}, u32[]{:S(2)}, u32[]{:S(2)}) collective-permute-start(bf16[256,1024]{1,0:T(8,128)(2,1)S(1)} %get-tuple-element.68), channel_id=1, source_target_pairs={{96,97},{97,96},{98,99},{99,98},{100,101},{101,100},{102,103},{103... | collective-permute-start | bytes 1572872 | tf_op jit(solution)/shard_map/ppermute | solution.py:31
  (39 other events, 241.3 us)
